TPU v7x, 512 devices: a whole 4x8x8 slice. The times are simulated.
512 devices in a mesh: dp: 16 (over x, z_lo), centre: 32 (over y, z_hi, core).
Axes of the slice: x: 4, y: 8, z: 8 (z_hi: 2, z_lo: 4; z = z_hi * 4 + z_lo), core: 2. Of those that a mesh axis runs over, the one named last changes fastest.
Arguments:
- samples: bfloat16 [524288, 256], P(('dp', 'centre')), may hold values from -9 to 9
- centres: bfloat16 [4096, 256], P('centre'), may hold values from -6 to 6
- factor: float32 [4096, 4096], P('centre'), as said below
- solution: float32 [4096], P('centre'), may hold values from -6 to 6
- residual: float32 [4096], P('centre'), may hold values from -6 to 6
- direction: float32 [4096], P('centre'), may hold values from -6 to 6
Outputs:
- new_solution: float32 [4096], P('centre')
- new_residual: float32 [4096], P('centre')
- new_direction: float32 [4096], P('centre')
Inputs may be any that keep to these rules, and one draw needn't show every extreme that they name: factor is upper triangular with a positive diagonal.
All inputs are finite; a program needn't handle non-finite values.
Results may differ from a plain program's by a relative error of at most 0.002.
Values may be sent and summed in bfloat16 or wider, within the bound.
A program may use at most 64 MiB of HBM per device.

v0:
```python
import math

import jax
import jax.numpy as jnp
from jax import lax
from jax.sharding import PartitionSpec as P

sharpness = 6.0
ridge = 0.3
balance = 16.0


def kernel_tile(rows, row_norms, cols):
    col_norms = jnp.sum(jnp.square(cols.astype(jnp.float32)), axis=1)
    cross = jnp.dot(rows, cols.T, preferred_element_type=jnp.float32)
    dist = row_norms[:, None] + col_norms[None, :] - 2.0 * cross
    return jnp.exp(sharpness * (2.0 - dist / rows.shape[1])).astype(jnp.bfloat16)


def tile_blocks(rows, row_norms, cols):
    col_total = cols.shape[0]
    part_width = math.gcd(col_total, 1024)
    turns = col_total // part_width

    def write_part(index, buffer):
        part_cols = lax.dynamic_slice_in_dim(cols, index * part_width, part_width, 0)
        return lax.dynamic_update_slice_in_dim(
            buffer, kernel_tile(rows, row_norms, part_cols), index * part_width, 1
        )

    blank = jnp.zeros((rows.shape[0], col_total), jnp.bfloat16)
    return lax.fori_loop(0, turns, write_part, blank)


def on_device(samples, centres, factor, solution, residual, direction):
    cycle_size = lax.axis_size("centre")
    group_size = lax.axis_size("dp")
    local_centres = centres.shape[0]
    total_centres = local_centres * cycle_size
    whole_dir = lax.all_gather(direction, "centre", axis=0, tiled=True)
    mapped = jnp.dot(factor, whole_dir, precision=lax.Precision.HIGHEST).astype(jnp.bfloat16)
    row_norms = jnp.sum(jnp.square(samples.astype(jnp.float32)), axis=1)
    part_centres = lax.all_gather(centres, "centre", axis=0, tiled=True)
    coeffs = lax.all_gather(mapped, "centre", axis=0, tiled=True)
    tile = tile_blocks(samples, row_norms, part_centres)
    total = jnp.dot(tile, coeffs, preferred_element_type=jnp.float32)
    total, tiles = (total, tile)
    weights = total.astype(jnp.bfloat16)
    column_part = lax.psum_scatter(
        jnp.dot(weights, tiles, preferred_element_type=jnp.float32),
        "centre",
        scatter_dimension=0,
        tiled=True,
    )
    columns = lax.psum(column_part, "dp")
    image_part = lax.psum_scatter(
        jnp.dot(columns, factor, precision=lax.Precision.HIGHEST),
        "centre",
        scatter_dimension=0,
        tiled=True,
    )
    total_samples = samples.shape[0] * group_size * cycle_size
    image = image_part / (balance * total_samples * math.sqrt(total_centres)) + ridge * direction
    old_norm, curvature = lax.psum(
        (jnp.sum(residual * residual), jnp.sum(direction * image)), "centre"
    )
    alpha = old_norm / curvature
    new_solution = solution + alpha * direction
    new_residual = residual - alpha * image
    new_norm = lax.psum(jnp.sum(new_residual * new_residual), "centre")
    new_direction = new_residual + new_norm / old_norm * direction
    return (new_solution, new_residual, new_direction)


def solution(mesh):
    return jax.shard_map(
        on_device,
        mesh=mesh,
        in_specs=(
            P(("dp", "centre"), None),
            P("centre", None),
            P("centre", None),
            P("centre"),
            P("centre"),
            P("centre"),
        ),
        out_specs=(P("centre"), P("centre"), P("centre")),
        check_vma=False,
    )
```

profile of v0, /device:TPU:1, one launch (start us, length us, event | category | flops | bytes accessed | tf_op | source)
XLA Modules:
  0.0 716.7 jit_solution(3432819644235342979)
XLA Ops:
  7.2 0.0 copy-start
  7.2 0.0 all-gather.4.cloned.1.call-start
  7.2 0.7 all-gather.4.cloned.1.call-update
  7.9 1.3 dynamic-slice
  9.8 59.2 %all-gather = f32[32,1,128]{2,1,0:T(1,128)S(1)} all-gather(f32[1,1,128]{2,1,0:T(1,128)} %bitcast.51), channel_id=1, replica_groups=mesh['dp'=16,'centre'=32] {'centre'}, dimensions={0}, use_global_device_ids=true | all-gather | bytes 16896 | tf_op jit(solution)/shard_map/all_gather | solution.py:40
  69.0 0.0 copy-done
  69.0 1.7 fusion.9
  70.7 46.3 %all-gather.1 = bf16[32,1,128]{2,1,0:T(2,128)(2,1)S(1)} all-gather(bf16[1,1,128]{2,1,0:T(2,128)(2,1)S(1)} %fusion.9), channel_id=1, replica_groups=mesh['dp'=16,'centre'=32] {'centre'}, dimensions={0}, use_global_device_ids=true | all-gather | bytes 8448 | tf_op jit(solution)/shard_map/all_gather | solution.py:44
  117.0 1.3 multiply_reduce_fusion.4
  118.3 1.3 multiply_reduce_fusion.1
  119.6 0.0 copy-start.2
  119.6 0.0 all-gather.4.cloned.1.call-done
  119.6 4.3 broadcast_in_dim.9
  123.9 0.0 copy-done.2
  123.9 20.0 %while.13 = (s32[]{:T(128)}, bf16[1024,4096]{0,1:T(8,128)(2,1)}, f32[1024]{0:T(1024)S(1)}, bf16[4096,256]{1,0:T(8,128)(2,1)}, bf16[1024,256]{1,0:T(8,128)(2,1)S(...) while((s32[]{:T(128)}, bf16[1024,4096]{0,1:T(8,128)(2,1)}, f32[1024]{0:T(1024)S(1)}, ...), condition=%wide.region_5.0_spmd, body=%wide.region_3.5_spmd.sunk | while | flops 544996352 | bytes 3683471 | solution.py:32
  123.9 1.3 multiply_reduce_fusion.6
  125.2 3.8 fusion.28
  128.9 1.3 multiply_reduce_fusion.6
  130.2 3.7 fusion.28
  133.9 1.3 multiply_reduce_fusion.6
  135.1 3.7 fusion.28
  138.9 1.3 multiply_reduce_fusion.6
  140.1 3.8 fusion.28
  143.9 0.0 copy-start.1
  143.9 4.7 fusion.10
  148.6 1.0 copy-done.1
  149.6 0.0 copy-start.3
  149.6 0.0 copy-start.5
  149.6 0.0 copy-start.6
  149.7 2.3 fusion.16
  151.9 164.2 %all-reduce = f32[4096]{0:T(1024)S(1)} all-reduce(f32[4096]{0:T(1024)S(1)} %bitcast.48), channel_id=2, replica_groups=mesh['dp'=16,'centre'=32] {'centre'}, use_global_device_ids=true, to_apply=%region_6.0.clone | all-reduce | flops 4096 | bytes 32768
  316.2 0.1 dynamic-slice.1
  316.2 36.4 %psum.29 = f32[128]{0:T(128)S(1)} all-reduce(f32[128]{0:T(128)S(1)} %dynamic-slice.1), channel_id=1, replica_groups=mesh['dp'=16,'centre'=32] {'dp'}, use_global_device_ids=true, to_apply=%region_7.0 | all-reduce | flops 128 | bytes 1024 | tf_op jit(solution)/shard_map/psum | solution.py:55
  352.7 1.1 fusion.14
  353.8 174.1 %all-reduce.1 = f32[4096]{0:T(1024)S(1)} all-reduce(f32[4096]{0:T(1024)S(1)} %bitcast.49), channel_id=3, replica_groups=mesh['dp'=16,'centre'=32] {'centre'}, use_global_device_ids=true, to_apply=%region_8.0.clone | all-reduce | flops 4096 | bytes 32768
  527.9 0.0 copy-done.3
  527.9 0.7 multiply_reduce_fusion.3
  528.6 92.5 %all-reduce.2 = (f32[]{:T(128)}, f32[]{:T(128)}) all-reduce(f32[]{:T(128)} %multiply_reduce_fusion.4, f32[]{:T(128)} %multiply_reduce_fusion.3), channel_id=1, replica_groups=mesh['dp'=16,'centre'=32] {'centre'}, use_global_device_ids=true, to_apply=%region_1.2 | all-reduce | flops 2 | bytes 16 | tf_op jit(solution)/shard_map/psum | solution.py:64
  622.4 0.0 copy-done.5
  622.4 0.7 multiply_reduce_fusion.2
  623.1 0.0 copy-start.4
  623.1 84.9 %psum.31 = f32[]{:T(128)} all-reduce(f32[]{:T(128)} %get-tuple-element.110), channel_id=1, replica_groups=mesh['dp'=16,'centre'=32] {'centre'}, use_global_device_ids=true, to_apply=%region_12.0 | all-reduce | flops 1 | bytes 8 | tf_op jit(solution)/shard_map/psum | solution.py:70
  709.3 0.0 copy-done.6
  709.3 0.5 multiply_add_fusion
  709.8 0.0 copy-done.4
  (2 shorter events, 0.0 us)
Async XLA Ops:
  7.2 61.9 %copy-start = (f32[128,4096]{1,0:T(8,128)S(1)}, f32[128,4096]{1,0:T(8,128)}, u32[]{:S(2)}) copy-start(f32[128,4096]{1,0:T(8,128)} %param.10) | copy-start | bytes 6291460
  7.2 112.4 %all-gather.4.cloned.1.call-start = ((), (), s32[]{:S(2)}) async-start(), calls=%async_computation | async-start | bytes 2162688 | tf_op jit(solution)/shard_map/all_gather | solution.py:43
  119.6 4.3 copy-start.2
  143.9 5.8 copy-start.1
  149.6 378.2 %copy-start.3 = (f32[128]{0:T(128)S(1)}, f32[128]{0:T(128)}, u32[]{:S(2)}) copy-start(f32[128]{0:T(128)} %param.13) | copy-start | bytes 1540
  149.6 472.7 %copy-start.5 = (f32[128]{0:T(128)S(1)}, f32[128]{0:T(128)}, u32[]{:S(2)}) copy-start(f32[128]{0:T(128)} %param.12) | copy-start | bytes 1540
  149.6 559.6 %copy-start.6 = (f32[128]{0:T(128)S(1)}, f32[128]{0:T(128)}, u32[]{:S(2)}) copy-start(f32[128]{0:T(128)} %param.11) | copy-start | bytes 1540
  623.1 86.7 %copy-start.4 = (f32[128]{0:T(128)}, f32[128]{0:T(128)S(1)}, u32[]{:S(2)}) copy-start(f32[128]{0:T(128)S(1)} %get-tuple-element.111) | copy-start | bytes 1540
Sparse Core Ops, SparseCore 0:
  11.4 100.1 all-gather.3
where the time goes:
time: 717 us
  blocking collectives  658 us (92%)
  matrix products  24.7 us (3%)
  between operations  17.4 us (2%)
  other arithmetic  9.4 us (1%)
    unnamed x2, blocking collectives  338 us
    psum x1, blocking collectives, on_device(): lax.psum((jnp.sum(residual * residual), jnp.sum(direction * image)), 'cen...  92.5 us
    psum x1, blocking collectives, on_device(): new_norm = lax.psum(jnp.sum(new_residual * new_residual), 'centre')  84.9 us
    all_gather x1, blocking collectives, on_device(): whole_dir = lax.all_gather(direction, 'centre', axis=0, tiled=True)  59.2 us
    all_gather x1, blocking collectives, on_device(): coeffs = lax.all_gather(mapped, 'centre', axis=0, tiled=True)  46.3 us
    psum x1, blocking collectives, on_device(): columns = lax.psum(column_part, 'dp')  36.4 us
    dot_general x4, matrix products, kernel_tile(): cross = jnp.dot(rows, cols.T, preferred_element_type=jnp.float32)  14.9 us
  transfers between devices with their start and end apart: 1, of which 0 were waited for; matrix products, arithmetic and copies ran while one was open for 1% of the time, Pallas kernels for 0%

commit v1 on v0

v1 whole, which is shorter than its diff:
```python
import functools
import math

import jax
import jax.numpy as jnp
from jax import lax
from jax.experimental import pallas as pl
from jax.experimental.pallas import tpu as pltpu
from jax.sharding import PartitionSpec as P

sharpness = 6.0
ridge = 0.3
balance = 16.0
MESH = pl.DeviceIdType.MESH
F32 = jnp.float32
BF16 = jnp.bfloat16


def step_kernel(
    n_dp,
    n_ce,
    scale,
    samples_hbm,
    centres_hbm,
    factor_hbm,
    sol_ref,
    res_ref,
    dir_ref,
    new_sol_ref,
    new_res_ref,
    new_dir_ref,
    smp,
    cen,
    fac,
    tiles,
    row_term,
    a_buf,
    m_buf,
    c_out,
    c_buf,
    g_buf,
    i_out,
    i_buf,
    e_buf,
    load_sem,
    cen_recv,
    cen_send,
    small_recv,
    small_send,
):
    dp = lax.axis_index("dp")
    me = lax.axis_index("centre")
    rows, depth = cen.shape[1], cen.shape[2]
    width = smp.shape[0]
    n_y = n_ce // 4
    n_tiles = n_ce // 2

    load_cen = pltpu.make_async_copy(centres_hbm, cen.at[me], load_sem.at[0])
    load_smp = pltpu.make_async_copy(samples_hbm, smp, load_sem.at[1])
    load_fac = pltpu.make_async_copy(factor_hbm, fac, load_sem.at[2])
    load_cen.start()
    load_smp.start()
    load_fac.start()

    barrier = pltpu.get_barrier_semaphore()

    @pl.loop(1, n_ce)
    def _(k):
        peer = lax.rem(me + k, n_ce)
        pl.semaphore_signal(barrier, inc=1, device_id=(dp, peer), device_id_type=MESH)

    @pl.loop(1, n_dp)
    def _(k):
        peer = lax.rem(dp + k, n_dp)
        pl.semaphore_signal(barrier, inc=1, device_id=(peer, me), device_id_type=MESH)

    residual = res_ref[...]
    direction = dir_ref[...]
    a_buf[me, :, 0:rows] = direction
    a_buf[me, :, rows : 2 * rows] = residual * residual
    pl.semaphore_wait(barrier, n_ce + n_dp - 2)

    def push_all(phase, source, landing):
        @pl.loop(1, n_ce)
        def _(k):
            peer = lax.rem(me + k, n_ce)
            pltpu.make_async_remote_copy(
                src_ref=source(peer),
                dst_ref=landing.at[me],
                send_sem=small_send.at[phase],
                recv_sem=small_recv.at[phase],
                device_id=(dp, peer),
                device_id_type=MESH,
            ).start()

    def wait_all(phase, landing, sems):
        part = landing.at[pl.ds(0, landing.shape[0] - 1)]
        pltpu.make_async_copy(part, part, sems.at[phase]).wait()

    def send_cen(slot, peer):
        pltpu.make_async_remote_copy(
            src_ref=cen.at[slot],
            dst_ref=cen.at[slot],
            send_sem=cen_send,
            recv_sem=cen_recv.at[slot],
            device_id=(dp, peer),
            device_id_type=MESH,
        ).start()

    def wait_cen(slot):
        pltpu.make_async_copy(cen.at[slot], cen.at[slot], cen_recv.at[slot]).wait()

    up = lax.rem(me + 4, n_ce)
    down = lax.rem(me + n_ce - 4, n_ce)
    core = lax.rem(me, 2)
    sibling = me + 1 - 2 * core
    half = lax.rem(me // 2, 2)
    across = me + 2 - 4 * half

    push_all(0, lambda peer: a_buf.at[me], a_buf)
    load_cen.wait()
    send_cen(me, up)
    send_cen(me, down)
    send_cen(me, across)
    send_cen(me, sibling)

    log2e = math.log2(math.e)
    unit = sharpness / depth * log2e

    load_smp.wait()
    for part in range(width // rows):
        block = smp[part * rows : (part + 1) * rows, :].astype(F32)
        square = block * block
        folded = square[:, 0:rows]
        for other in range(1, depth // rows):
            folded = folded + square[:, other * rows : (other + 1) * rows]
        norms = jnp.sum(folded.T, axis=0, keepdims=True)
        row_term[:, part * rows : (part + 1) * rows] = (2.0 * sharpness * log2e) - unit * norms

    def make_tile(tile):
        block = cen[pl.ds(2 * tile, 2)].reshape(2 * rows, depth)
        wide = block.astype(F32)
        norms = jnp.sum(wide * wide, axis=1, keepdims=True) * unit
        cross = lax.dot_general(
            block, smp[...], (((1,), (1,)), ((), ())), preferred_element_type=F32
        )
        power = cross * (2.0 * unit) + (row_term[...] - norms)
        tiles[tile] = jnp.exp2(power).astype(BF16)

    wait_cen(sibling)
    make_tile(me // 2)

    load_fac.wait()
    wait_all(0, a_buf, small_recv)
    acc = fac[:, 0:rows] * a_buf[0, :, 0:rows]
    for b in range(1, n_ce):
        acc = acc + fac[:, b * rows : (b + 1) * rows] * a_buf[b, :, 0:rows]
    m_buf[me] = jnp.sum(acc.T, axis=0, keepdims=True)
    push_all(1, lambda peer: m_buf.at[me], m_buf)

    wait_cen(across)
    send_cen(across, up)
    send_cen(across, down)
    send_cen(across, sibling)
    wait_cen(across + 1 - 2 * core)
    make_tile(across // 2)

    @pl.loop(1, n_y // 2)
    def _(s):
        for first in (me, across):
            low = lax.rem(first + n_ce - 4 * s, n_ce)
            high = lax.rem(first + 4 * s, n_ce)
            wait_cen(low)
            send_cen(low, up)
            send_cen(low, sibling)
            wait_cen(high)

            @pl.when(s < n_y // 2 - 1)
            def _():
                send_cen(high, down)

            send_cen(high, sibling)
            wait_cen(low + 1 - 2 * core)
            make_tile(low // 2)
            wait_cen(high + 1 - 2 * core)
            make_tile(high // 2)

    for first in (me, across):
        far = lax.rem(first + n_ce // 2, n_ce)
        wait_cen(far)
        send_cen(far, sibling)
        wait_cen(far + 1 - 2 * core)
        make_tile(far // 2)

    wait_all(1, m_buf, small_recv)

    def add_weights(tile, total):
        coeffs = jnp.concatenate([m_buf[2 * tile], m_buf[2 * tile + 1]], axis=1)
        coeffs = jnp.broadcast_to(coeffs, (16, 2 * rows)).astype(BF16)
        return total + jnp.dot(coeffs, tiles[tile], preferred_element_type=F32)

    weights = lax.fori_loop(0, n_tiles, add_weights, jnp.zeros((16, width), F32)).astype(BF16)

    @pl.loop(0, n_tiles)
    def _(tile):
        part = lax.dot_general(
            weights, tiles[tile], (((1,), (1,)), ((), ())), preferred_element_type=F32
        )
        c_out[2 * tile] = part[0:1, 0:rows]
        c_out[2 * tile + 1] = part[0:1, rows : 2 * rows]

    c_buf[me] = c_out[me]
    push_all(2, lambda peer: c_out.at[peer], c_buf)
    wait_all(2, c_buf, small_recv)
    g_buf[dp] = jnp.sum(c_buf[...], axis=0)

    @pl.loop(1, n_dp)
    def _(k):
        peer = lax.rem(dp + k, n_dp)
        pltpu.make_async_remote_copy(
            src_ref=g_buf.at[dp],
            dst_ref=g_buf.at[dp],
            send_sem=small_send.at[3],
            recv_sem=small_recv.at[3],
            device_id=(peer, me),
            device_id_type=MESH,
        ).start()

    wait_all(3, g_buf, small_recv)
    columns = jnp.sum(g_buf[...], axis=0) * scale

    spread = jnp.broadcast_to(columns, (rows, rows)).T
    bend = m_buf[me] * columns
    for b in range(n_ce):
        i_out[b, :, 0:rows] = jnp.sum(
            fac[:, b * rows : (b + 1) * rows] * spread, axis=0, keepdims=True
        )
        i_out[b, :, rows : 2 * rows] = bend
    i_buf[me] = i_out[me]
    push_all(4, lambda peer: i_out.at[peer], i_buf)
    gathered = jnp.sum(a_buf[:, :, rows : 2 * rows], axis=0)
    old_norm = jnp.sum(gathered, axis=1, keepdims=True)
    whole = a_buf[:, :, 0:rows]
    dir_norm = jnp.sum(jnp.sum(whole * whole, axis=0), axis=1, keepdims=True)
    wait_all(4, i_buf, small_recv)
    both = jnp.sum(i_buf[...], axis=0)
    image = both[:, 0:rows] + ridge * direction
    curvature = jnp.sum(both[:, rows : 2 * rows], axis=1, keepdims=True) + ridge * dir_norm
    alpha = old_norm / curvature
    new_residual = residual - alpha * image
    e_buf[me] = new_residual * new_residual
    push_all(5, lambda peer: e_buf.at[me], e_buf)
    new_sol_ref[...] = sol_ref[...] + alpha * direction
    new_res_ref[...] = new_residual
    wait_all(5, e_buf, small_recv)
    new_norm = jnp.sum(jnp.sum(e_buf[...], axis=0), axis=1, keepdims=True)
    new_dir_ref[...] = new_residual + new_norm / old_norm * direction

    for phase, landing in ((0, a_buf), (1, m_buf), (2, c_buf), (3, g_buf), (4, i_buf), (5, e_buf)):
        wait_all(phase, landing, small_send)
    sent = cen.at[pl.ds(0, n_ce - 1)]
    pltpu.make_async_copy(sent, sent, cen_send).wait()


def on_device(n_dp, n_ce, samples, centres, factor, solution, residual, direction):
    rows, depth = centres.shape
    width = samples.shape[0]
    total_samples = width * n_dp * n_ce
    scale = 1.0 / (balance * total_samples * math.sqrt(rows * n_ce))
    vector = jax.ShapeDtypeStruct((1, rows), F32)
    vmem = pl.BlockSpec(memory_space=pltpu.VMEM)
    anywhere = pl.BlockSpec(memory_space=pl.ANY)
    outs = pl.pallas_call(
        functools.partial(step_kernel, n_dp, n_ce, scale),
        out_shape=(vector, vector, vector),
        in_specs=[anywhere, anywhere, anywhere, vmem, vmem, vmem],
        out_specs=(vmem, vmem, vmem),
        scratch_shapes=[
            pltpu.VMEM((width, depth), BF16),
            pltpu.VMEM((n_ce, rows, depth), BF16),
            pltpu.VMEM((rows, rows * n_ce), F32),
            pltpu.VMEM((n_ce // 2, 2 * rows, width), BF16),
            pltpu.VMEM((1, width), F32),
            pltpu.VMEM((n_ce, 1, 2 * rows), F32),
            pltpu.VMEM((n_ce, 1, rows), F32),
            pltpu.VMEM((n_ce, 1, rows), F32),
            pltpu.VMEM((n_ce, 1, rows), F32),
            pltpu.VMEM((n_dp, 1, rows), F32),
            pltpu.VMEM((n_ce, 1, 2 * rows), F32),
            pltpu.VMEM((n_ce, 1, 2 * rows), F32),
            pltpu.VMEM((n_ce, 1, rows), F32),
            pltpu.SemaphoreType.DMA((3,)),
            pltpu.SemaphoreType.DMA((n_ce,)),
            pltpu.SemaphoreType.DMA,
            pltpu.SemaphoreType.DMA((6,)),
            pltpu.SemaphoreType.DMA((6,)),
        ],
        compiler_params=pltpu.CompilerParams(
            collective_id=0, has_side_effects=True, vmem_limit_bytes=40 * 1024 * 1024
        ),
        cost_estimate=pl.CostEstimate(
            flops=2 * width * rows * n_ce * (depth + 2),
            bytes_accessed=4 * rows * rows * n_ce,
            transcendentals=width * rows * n_ce,
        ),
    )(
        samples,
        centres,
        factor,
        solution.reshape(1, rows),
        residual.reshape(1, rows),
        direction.reshape(1, rows),
    )
    return tuple(out.reshape(rows) for out in outs)


def solution(mesh):
    return jax.shard_map(
        functools.partial(on_device, mesh.shape["dp"], mesh.shape["centre"]),
        mesh=mesh,
        in_specs=(
            P(("dp", "centre"), None),
            P("centre", None),
            P("centre", None),
            P("centre"),
            P("centre"),
            P("centre"),
        ),
        out_specs=(P("centre"), P("centre"), P("centre")),
        check_vma=False,
    )
```

time: 717 us -> 84.8 us (0.12)
  blocking collectives: 658 us -> 0 us
  Pallas kernels: 0 us -> 76.9 us
  matrix products: 24.7 us -> 0 us
  between operations: 17.4 us -> 0.65 us
  other arithmetic: 9.4 us -> 0 us
    unnamed x2 -> x0, blocking collectives: 338 us -> none
    psum x3 -> x0, blocking collectives: 214 us -> none  [the longest x1 92.5 us: on_device(): lax.psum((jnp.sum(residual * residual), jnp.sum(direction * image)), 'cen...]
    all_gather x2 -> x0, blocking collectives: 105 us -> none  [the longest x1 59.2 us: on_device(): whole_dir = lax.all_gather(direction, 'centre', axis=0, tiled=True)]
    pallas_call x0 -> x1, Pallas kernels: none -> 76.9 us  [on_device(): pl.pallas_call(functools.partial(step_kernel, n_dp, n_ce, scale), out_sha...]
    dot_general x8 -> x0, matrix products: 24.7 us -> none  [the longest x4 14.9 us: kernel_tile(): cross = jnp.dot(rows, cols.T, preferred_element_type=jnp.float32)]
    reduce_sum x8 -> x0, other arithmetic: 8.87 us -> none  [the longest x4 5.01 us: kernel_tile(): col_norms = jnp.sum(jnp.square(cols.astype(jnp.float32)), axis=1)]
  transfers between devices with their start and end apart: 1 -> 0, of which waited for: 0 -> 0; matrix products, arithmetic and copies ran while one was open for 1% -> 0% of each run, Pallas kernels for 0% -> 0%
where the time goes in v1:
time: 84.8 us; the launch traced here: 84.5 us
  Pallas kernels  76.9 us (91%)
  local copies, waits for them, and re-layouts  6.96 us (8%)
    pallas_call x1, Pallas kernels, on_device(): pl.pallas_call(functools.partial(step_kernel, n_dp, n_ce, scale), out_sha...  76.9 us
    unnamed x15, local copies, waits for them, and re-layouts  6.96 us

profile of v1, /device:TPU:1, one launch (start us, length us, event | category | flops | bytes accessed | tf_op | source)
XLA Modules:
  0.0 84.5 jit_solution(2737286032578272355)
XLA Ops:
  0.6 0.0 copy-start
  0.6 1.6 %copy-done = f32[128,4096]{1,0:T(8,128)S(1)} copy-done((f32[128,4096]{1,0:T(8,128)S(1)}, f32[128,4096]{1,0:T(8,128)}, u32[]{:S(2)}) %copy-start) | copy-done | bytes 2097176
  2.2 0.0 copy-start.1
  2.2 1.0 %copy-done.1 = bf16[1024,256]{1,0:T(8,128)(2,1)S(1)} copy-done((bf16[1024,256]{1,0:T(8,128)(2,1)S(1)}, bf16[1024,256]{1,0:T(8,128)(2,1)}, u32[]{:S(2)}) %copy-start.1) | copy-done | bytes 524312
  3.3 0.0 copy-start.2
  3.3 0.8 copy-done.2
  4.1 0.0 copy-start.3
  4.1 0.7 copy-done.3
  4.8 0.0 copy-start.4
  4.8 0.7 copy-done.4
  5.4 0.0 copy-start.5
  5.4 0.7 copy-done.5
  6.1 76.9 %shard_map.85 = (f32[1,128]{1,0:T(1,128)S(1)}, f32[1,128]{1,0:T(1,128)S(1)}, f32[1,128]{1,0:T(1,128)S(1)}) custom-call(bf16[1024,256]{1,0:T(8,128)(2,1)S(1)} %copy-done.1, bf16[128,256]{1,0:T(8,128)(2,1)S(1)} %copy-done.2, f32[128,4096]{1,0:T(8,128)S(1)} %copy-done, f32[1,128]{1,0:T(1,128)S(1)} %bitcast.6, f32[1,128]{1,0:T(1,128)S(1)} %bitcast.7, ...), custom_call_target="tpu_custom_call" | custom-call | flops 2164260864 | bytes 2097152 | tf_op jit(solution)/shard_map/pallas_call | solution.py:273
  83.0 0.5 copy.12
  83.5 0.5 copy.13
  84.0 0.5 copy.14
Async XLA Ops:
  0.6 1.6 %copy-start = (f32[128,4096]{1,0:T(8,128)S(1)}, f32[128,4096]{1,0:T(8,128)}, u32[]{:S(2)}) copy-start(f32[128,4096]{1,0:T(8,128)} %factor_hbm.1) | copy-start | bytes 6291460
  2.2 1.0 %copy-start.1 = (bf16[1024,256]{1,0:T(8,128)(2,1)S(1)}, bf16[1024,256]{1,0:T(8,128)(2,1)}, u32[]{:S(2)}) copy-start(bf16[1024,256]{1,0:T(8,128)(2,1)} %samples_hbm.1) | copy-start | bytes 1572868
  3.3 0.8 copy-start.2
  4.1 0.7 copy-start.3
  4.8 0.7 copy-start.4
  5.4 0.7 copy-start.5

commit v2 on v1

v2 whole, which is shorter than its diff:
```python
import functools
import math

import jax
import jax.numpy as jnp
from jax import lax
from jax.experimental import pallas as pl
from jax.experimental.pallas import tpu as pltpu
from jax.sharding import PartitionSpec as P

sharpness = 6.0
ridge = 0.3
balance = 16.0
z_low = 4
MESH = pl.DeviceIdType.MESH
F32 = jnp.float32
BF16 = jnp.bfloat16


def step_kernel(
    n_dp,
    n_ce,
    scale,
    samples_hbm,
    centres_hbm,
    factor_hbm,
    res_hbm,
    dir_hbm,
    out_ref,
    smp,
    cen,
    fac,
    res_ref,
    dir_ref,
    tiles,
    row_term,
    a_buf,
    m_buf,
    c_out,
    c_buf,
    g_out,
    g_buf,
    i_out,
    i_buf,
    e_buf,
    left_ref,
    load_sem,
    cen_recv,
    cen_send,
    small_recv,
    small_send,
    token,
):
    dp = lax.axis_index("dp")
    me = lax.axis_index("centre")
    rows, depth = cen.shape[1], cen.shape[2]
    width = smp.shape[0]
    n_y = n_ce // 4
    n_q = 2 * n_y
    n_x = n_dp // z_low
    n_z = 2 * z_low
    n_p = n_x * n_z
    n_tiles = n_ce // 2
    x, low_z = dp // z_low, lax.rem(dp, z_low)
    y, half, core = me // 4, lax.rem(me // 2, 2), lax.rem(me, 2)
    z = half * z_low + low_z
    mine = y * 2 + core
    place = x * n_z + z

    def column_peer(k):
        q = lax.rem(mine + k, n_q)
        return q, (dp, (q // 2) * 4 + half * 2 + lax.rem(q, 2))

    def z_peer(k):
        other = lax.rem(z + k, n_z)
        return (x * z_low + lax.rem(other, z_low), y * 4 + (other // z_low) * 2 + core)

    def plane_peer(k):
        p = lax.rem(place + k, n_p)
        other = lax.rem(p, n_z)
        there = (p // n_z) * z_low + lax.rem(other, z_low)
        return other // z_low, (there, y * 4 + (other // z_low) * 2 + core)

    def group_peer(k):
        peer = lax.rem(me + k, n_ce)
        return (peer // 4) * 2 + lax.rem(peer, 2), (dp, peer)

    up = lax.rem(me + 4, n_ce)
    down = lax.rem(me + n_ce - 4, n_ce)
    sibling = me + 1 - 2 * core
    across = me + 2 - 4 * half

    loads = [
        pltpu.make_async_copy(dir_hbm, dir_ref, load_sem.at[0]),
        pltpu.make_async_copy(res_hbm, res_ref, load_sem.at[1]),
        pltpu.make_async_copy(centres_hbm, cen.at[me], load_sem.at[2]),
        pltpu.make_async_copy(samples_hbm, smp, load_sem.at[3]),
        pltpu.make_async_copy(factor_hbm, fac, load_sem.at[4]),
    ]
    for load in loads:
        load.start()

    barrier = pltpu.get_barrier_semaphore()

    @pl.loop(1, n_q)
    def _(k):
        pl.semaphore_signal(barrier, inc=1, device_id=column_peer(k)[1], device_id_type=MESH)

    @pl.loop(1, n_z)
    def _(k):
        pl.semaphore_signal(barrier, inc=1, device_id=z_peer(k), device_id_type=MESH)

    @pl.loop(1, n_x)
    def _(k):
        peer = lax.rem(x + k, n_x) * z_low + low_z
        pl.semaphore_signal(barrier, inc=1, device_id=(peer, me), device_id_type=MESH)

    def copy_small(source, target, slot, device):
        pltpu.make_async_remote_copy(
            src_ref=source,
            dst_ref=target,
            send_sem=small_send.at[slot],
            recv_sem=small_recv.at[slot],
            device_id=device,
            device_id_type=MESH,
        ).start()

    def wait_small(landing, count, slot, sems):
        part = landing.at[pl.ds(0, count)]
        pltpu.make_async_copy(part, part, sems.at[slot]).wait()

    def send_cen(slot, peer, part=slice(None), sem=None):
        pltpu.make_async_remote_copy(
            src_ref=cen.at[slot, part],
            dst_ref=cen.at[slot, part],
            send_sem=cen_send,
            recv_sem=cen_recv.at[slot if sem is None else sem],
            device_id=(dp, peer),
            device_id_type=MESH,
        ).start()

    def wait_cen(slot, part=slice(None), sem=None):
        landed = cen.at[slot, part]
        pltpu.make_async_copy(
            landed, landed, cen_recv.at[slot if sem is None else sem]
        ).wait()

    loads[0].wait()
    loads[1].wait()
    a_buf[me, :, 0:rows] = dir_ref[...]
    a_buf[me, :, rows : 2 * rows] = res_ref[...]
    loads[2].wait()

    log2e = math.log2(math.e)
    unit = sharpness / depth * log2e
    loads[3].wait()
    for part in range(width // rows):
        block = smp[part * rows : (part + 1) * rows, :].astype(F32)
        square = block * block
        folded = square[:, 0:rows]
        for other in range(1, depth // rows):
            folded = folded + square[:, other * rows : (other + 1) * rows]
        norms = jnp.sum(folded.T, axis=0, keepdims=True)
        row_term[:, part * rows : (part + 1) * rows] = (2.0 * sharpness * log2e) - unit * norms

    pl.semaphore_wait(barrier, n_q + n_z + n_x - 3)

    copy_small(a_buf.at[me], a_buf.at[me], 1, (dp, across))

    @pl.loop(1, n_q)
    def _(k):
        copy_small(a_buf.at[me], a_buf.at[me], 0, column_peer(k)[1])

    send_cen(me, across)
    send_cen(me, up)
    send_cen(me, down)
    send_cen(me, sibling)

    @pl.loop(1, n_z)
    def _(k):
        pl.semaphore_signal(token, inc=1, device_id=z_peer(k), device_id_type=MESH)

    def make_tile(slot):
        tile = slot // 2
        block = cen[pl.ds(2 * tile, 2)].reshape(2 * rows, depth)
        wide = block.astype(F32)
        norms = jnp.sum(wide * wide, axis=1, keepdims=True) * unit
        cross = lax.dot_general(
            block, smp[...], (((1,), (1,)), ((), ())), preferred_element_type=F32
        )
        power = cross * (2.0 * unit) + (row_term[...] - norms)
        tiles[tile] = jnp.exp2(power).astype(BF16)

    def twin(slot):
        return slot + 1 - 2 * core

    def pull(first, s):
        low = lax.rem(first + n_ce - 4 * s, n_ce)
        high = lax.rem(first + 4 * s, n_ce)
        wait_cen(low)
        if s < n_y // 2 - 1:
            send_cen(low, up)
        else:
            send_cen(low, up, top)
        send_cen(low, sibling)
        wait_cen(high)
        if s < n_y // 2 - 1:
            send_cen(high, down)
        else:
            send_cen(high, down, bottom, n_ce + far_sem[first is across])
        send_cen(high, sibling)
        return [low, high]

    def pull_far(first):
        far = lax.rem(first + n_ce // 2, n_ce)
        wait_cen(far, top)
        wait_cen(far, bottom, n_ce + far_sem[first is across])
        send_cen(far, sibling)
        return [far]

    top, bottom = slice(0, rows // 2), slice(rows // 2, rows)
    far_sem = {False: 0, True: 1}

    def work(slots):
        for slot in slots:
            wait_cen(twin(slot))
            make_tile(slot)

    work([me])
    wait_small(a_buf, 1, 1, small_recv)

    @pl.loop(1, n_q)
    def _(k):
        copy_small(a_buf.at[across], a_buf.at[across], 2, column_peer(k)[1])

    near = pull(me, 1)
    wait_cen(across)
    send_cen(across, up)
    send_cen(across, down)
    send_cen(across, sibling)
    work(near)
    next_own = pull(me, 2)
    work([across])
    next_far = pull(across, 1)
    work(next_own)

    wait_small(a_buf, n_q - 1, 0, small_recv)
    wait_small(a_buf, n_q - 1, 2, small_recv)
    loads[4].wait()
    acc = fac[:, 0:rows] * a_buf[0, :, 0:rows]
    for b in range(1, n_ce):
        acc = acc + fac[:, b * rows : (b + 1) * rows] * a_buf[b, :, 0:rows]
    m_buf[me] = jnp.sum(acc.T, axis=0, keepdims=True)

    @pl.loop(1, n_ce)
    def _(k):
        copy_small(m_buf.at[me], m_buf.at[me], 3, group_peer(k)[1])

    next_own = pull(me, 3)
    work(next_far)
    next_far = pull(across, 2)
    work(next_own)
    next_own = pull_far(me)
    work(next_far)
    next_far = pull(across, 3)
    work(next_own)
    work(next_far)
    work(pull_far(across))

    wait_small(m_buf, n_ce - 1, 3, small_recv)

    def add_weights(tile, total):
        coeffs = jnp.concatenate([m_buf[2 * tile], m_buf[2 * tile + 1]], axis=1)
        coeffs = jnp.broadcast_to(coeffs, (16, 2 * rows)).astype(BF16)
        return total + jnp.dot(coeffs, tiles[tile], preferred_element_type=F32)

    weights = lax.fori_loop(0, n_tiles, add_weights, jnp.zeros((16, width), F32))
    upright = jnp.broadcast_to(weights[0:1], (rows, width)).T.astype(BF16)
    diagonal = lax.broadcasted_iota(jnp.int32, (rows, rows), 0) == lax.broadcasted_iota(
        jnp.int32, (rows, rows), 1
    )

    @pl.loop(0, n_y)
    def _(row):
        for side in range(2):
            part = jnp.dot(tiles[2 * row + side], upright, preferred_element_type=F32)
            for c in range(2):
                picked = jnp.where(diagonal, part[c * rows : (c + 1) * rows], 0.0)
                c_out[2 * row + c, :, side * rows : (side + 1) * rows] = jnp.sum(
                    picked, axis=0, keepdims=True
                )

    c_buf[mine] = c_out[mine]

    @pl.loop(1, n_q)
    def _(k):
        q, device = column_peer(k)
        copy_small(c_out.at[q], c_buf.at[mine], 4, device)

    wait_small(c_buf, n_q - 1, 4, small_recv)
    both = jnp.sum(c_buf[...], axis=0)
    g_out[0] = both[:, 0:rows]
    g_out[1] = both[:, rows : 2 * rows]
    pl.semaphore_wait(token, n_z - 1)

    @pl.loop(1, n_p)
    def _(k):
        side, device = plane_peer(k)
        copy_small(g_out.at[side], g_buf.at[place], 5, device)

    g_buf[place] = g_out[half]
    wait_small(g_buf, n_p - 1, 5, small_recv)
    columns = jnp.sum(g_buf[...], axis=0) * scale

    spread = jnp.broadcast_to(columns, (rows, rows)).T
    bend = m_buf[me] * columns
    for b in range(n_ce):
        q, side = (b // 4) * 2 + b % 2, (b // 2) % 2
        i_out[q, :, side * rows : (side + 1) * rows] = jnp.sum(
            fac[:, b * rows : (b + 1) * rows] * spread, axis=0, keepdims=True
        )
        if side == 0:
            i_out[q, :, 2 * rows : 3 * rows] = bend

    @pl.loop(1, n_ce)
    def _(k):
        q, device = group_peer(k)
        copy_small(i_out.at[q], i_buf.at[me], 6, device)

    i_buf[me] = i_out[mine]
    whole_dir = a_buf[:, :, 0:rows]
    whole_res = a_buf[:, :, rows : 2 * rows]
    dir_norm = jnp.sum(jnp.sum(whole_dir * whole_dir, axis=0), axis=1, keepdims=True)
    old_norm = jnp.sum(jnp.sum(whole_res * whole_res, axis=0), axis=1, keepdims=True)
    pair = me - 2 * half
    wait_small(i_buf, n_ce - 1, 6, small_recv)
    summed = jnp.sum(i_buf[...], axis=0)
    curvature = jnp.sum(summed[:, 2 * rows :], axis=1, keepdims=True) + ridge * dir_norm
    alpha = old_norm / curvature
    squares = jnp.zeros((1, rows), F32)
    for side in range(2):
        own_dir = a_buf[pair + 2 * side, :, 0:rows]
        image = summed[:, side * rows : (side + 1) * rows] + ridge * own_dir
        left = a_buf[pair + 2 * side, :, rows : 2 * rows] - alpha * image
        squares = squares + left * left
        left_ref[side] = left
    e_buf[mine] = squares

    @pl.loop(1, n_q)
    def _(k):
        copy_small(e_buf.at[mine], e_buf.at[mine], 7, column_peer(k)[1])

    out_ref[0:1, :] = jnp.broadcast_to(alpha, (1, rows))
    out_ref[1:2, :] = left_ref[half]
    wait_small(e_buf, n_q - 1, 7, small_recv)
    new_norm = jnp.sum(jnp.sum(e_buf[...], axis=0), axis=1, keepdims=True)
    out_ref[2:3, :] = jnp.broadcast_to(new_norm / old_norm, (1, rows))

    for slot, landing, count in (
        (0, a_buf, n_q - 1),
        (1, a_buf, 1),
        (2, a_buf, n_q - 1),
        (3, m_buf, n_ce - 1),
        (4, c_buf, n_q - 1),
        (5, g_buf, n_p - 1),
        (6, i_buf, n_ce - 1),
        (7, e_buf, n_q - 1),
    ):
        wait_small(landing, count, slot, small_send)
    sent = cen.at[pl.ds(0, n_ce - 1)]
    pltpu.make_async_copy(sent, sent, cen_send).wait()


def on_device(n_dp, n_ce, samples, centres, factor, solution, residual, direction):
    rows, depth = centres.shape
    width = samples.shape[0]
    total_samples = width * n_dp * n_ce
    scale = 1.0 / (balance * total_samples * math.sqrt(rows * n_ce))
    hbm = pl.BlockSpec(memory_space=pltpu.HBM)
    n_q = n_ce // 2
    n_p = 2 * n_dp
    out = pl.pallas_call(
        functools.partial(step_kernel, n_dp, n_ce, scale),
        out_shape=jax.ShapeDtypeStruct((8, rows), F32),
        in_specs=[hbm] * 5,
        out_specs=pl.BlockSpec(memory_space=pltpu.VMEM),
        scratch_shapes=[
            pltpu.VMEM((width, depth), BF16),
            pltpu.VMEM((n_ce, rows, depth), BF16),
            pltpu.VMEM((rows, rows * n_ce), F32),
            pltpu.VMEM((1, rows), F32),
            pltpu.VMEM((1, rows), F32),
            pltpu.VMEM((n_ce // 2, 2 * rows, width), BF16),
            pltpu.VMEM((1, width), F32),
            pltpu.VMEM((n_ce, 1, 2 * rows), F32),
            pltpu.VMEM((n_ce, 1, rows), F32),
            pltpu.VMEM((n_q, 1, 2 * rows), F32),
            pltpu.VMEM((n_q, 1, 2 * rows), F32),
            pltpu.VMEM((2, 1, rows), F32),
            pltpu.VMEM((n_p, 1, rows), F32),
            pltpu.VMEM((n_q, 1, 3 * rows), F32),
            pltpu.VMEM((n_ce, 1, 3 * rows), F32),
            pltpu.VMEM((n_q, 1, rows), F32),
            pltpu.VMEM((2, 1, rows), F32),
            pltpu.SemaphoreType.DMA((5,)),
            pltpu.SemaphoreType.DMA((n_ce + 2,)),
            pltpu.SemaphoreType.DMA,
            pltpu.SemaphoreType.DMA((8,)),
            pltpu.SemaphoreType.DMA((8,)),
            pltpu.SemaphoreType.REGULAR,
        ],
        compiler_params=pltpu.CompilerParams(
            collective_id=0, has_side_effects=True, vmem_limit_bytes=63 * 1024 * 1024
        ),
        cost_estimate=pl.CostEstimate(
            flops=2 * width * rows * n_ce * (depth + 2),
            bytes_accessed=4 * rows * rows * n_ce,
            transcendentals=width * rows * n_ce,
        ),
    )(samples, centres, factor, residual.reshape(1, rows), direction.reshape(1, rows))
    alpha, new_residual, ratio = out[0], out[1], out[2]
    return (solution + alpha * direction, new_residual, new_residual + ratio * direction)


def solution(mesh):
    return jax.shard_map(
        functools.partial(on_device, mesh.shape["dp"], mesh.shape["centre"]),
        mesh=mesh,
        in_specs=(
            P(("dp", "centre"), None),
            P("centre", None),
            P("centre", None),
            P("centre"),
            P("centre"),
            P("centre"),
        ),
        out_specs=(P("centre"), P("centre"), P("centre")),
        check_vma=False,
    )
```

time: 84.8 us -> 70.2 us (0.83)
  Pallas kernels: 76.9 us -> 68 us
  local copies, waits for them, and re-layouts: 6.96 us -> 0.01 us
  other arithmetic: 0 us -> 1.31 us
    pallas_call x1, Pallas kernels: 76.9 us -> 68 us  [on_device(): pl.pallas_call(functools.partial(step_kernel, n_dp, n_ce, scale), out_sha...]
    unnamed x15 -> x4, local copies, waits for them, and re-layouts: 6.96 us -> 0.01 us
    add x0 -> x1, other arithmetic: none -> 1.31 us  [on_device(): new_residual + ratio * direction]
where the time goes in v2:
time: 70.2 us; the launch traced here: 70 us
  Pallas kernels  68 us (97%)
  other arithmetic  1.31 us (2%)
    pallas_call x1, Pallas kernels, on_device(): pl.pallas_call(functools.partial(step_kernel, n_dp, n_ce, scale), out_sha...  68 us

profile of v2, /device:TPU:1, one launch (start us, length us, event | category | flops | bytes accessed | tf_op | source)
XLA Modules:
  0.0 70.0 jit_solution(11240452583994528135)
XLA Ops:
  0.6 0.0 copy-start
  0.6 0.0 copy-start.1
  0.7 68.0 %shard_map.85 = f32[8,128]{1,0:T(8,128)} custom-call(bf16[1024,256]{1,0:T(8,128)(2,1)} %samples_hbm.1, bf16[128,256]{1,0:T(8,128)(2,1)} %centres_hbm.1, f32[128,4096]{1,0:T(8,128)} %factor_hbm.1, f32[1,128]{1,0:T(1,128)} %bitcast.14, f32[1,128]{1,0:T(1,128)} %bitcast.13), custom_call_target="tpu_custom_call" | custom-call | flops 2164260864 | bytes 2097152 | tf_op jit(solution)/shard_map/pallas_call | solution.py:382
  68.7 0.0 copy-done
  68.7 0.0 copy-done.1
  68.7 1.3 %fusion = (f32[128]{0:T(128)}, f32[128]{0:T(128)}, f32[128]{0:T(128)}) fusion(f32[128]{0:T(128)S(1)} %copy-done, f32[8,128]{1,0:T(8,128)} %shard_map.85, f32[128]{0:T(128)S(1)} %copy-done.1), kind=kLoop, calls=%fused_computation.1 | loop fusion | flops 512 | bytes 4096 | tf_op jit(solution)/shard_map/add | solution.py:422
Async XLA Ops:
  0.6 68.1 %copy-start = (f32[128]{0:T(128)S(1)}, f32[128]{0:T(128)}, u32[]{:S(2)}) copy-start(f32[128]{0:T(128)} %param.11) | copy-start | bytes 1540
  0.6 68.1 %copy-start.1 = (f32[128]{0:T(128)S(1)}, f32[128]{0:T(128)}, u32[]{:S(2)}) copy-start(f32[128]{0:T(128)} %param.9) | copy-start | bytes 1540

commit v3 on v2

--- a/solution.py
+++ b/solution.py
@@ -12,6 +12,7 @@
 ridge = 0.3
 balance = 16.0
 z_low = 4
+EDGES = True
 MESH = pl.DeviceIdType.MESH
 F32 = jnp.float32
 BF16 = jnp.bfloat16
@@ -44,6 +45,7 @@
     i_buf,
     e_buf,
     left_ref,
+    w_acc,
     load_sem,
     cen_recv,
     cen_send,
@@ -90,6 +92,11 @@
     sibling = me + 1 - 2 * core
     across = me + 2 - 4 * half
 
+    at_edge = (low_z == 0) | (low_z == z_low - 1)
+    first_low = jnp.where(low_z == 0, z_low - 1, 0)
+    second_low = jnp.where(low_z == 0, z_low - 2, 1)
+    served = [x * z_low + first_low, x * z_low + second_low]
+
     loads = [
         pltpu.make_async_copy(dir_hbm, dir_ref, load_sem.at[0]),
         pltpu.make_async_copy(res_hbm, res_ref, load_sem.at[1]),
@@ -129,13 +136,36 @@
         part = landing.at[pl.ds(0, count)]
         pltpu.make_async_copy(part, part, sems.at[slot]).wait()
 
-    def send_cen(slot, peer, part=slice(None), sem=None):
+    def push_group(slot, source, landing):
+        if EDGES:
+            @pl.when(at_edge)
+            def _():
+                for there in served:
+
+                    @pl.loop(0, n_q)
+                    def _(k):
+                        q = lax.rem(mine + k + n_q // 2, n_q)
+                        peer = (q // 2) * 4 + (1 - half) * 2 + lax.rem(q, 2)
+                        copy_small(source(q), landing.at[me], slot, (there, peer))
+
+            @pl.loop(1, n_q)
+            def _(k):
+                q, device = column_peer(k)
+                copy_small(source(q), landing.at[me], slot, device)
+        else:
+
+            @pl.loop(1, n_ce)
+            def _(k):
+                q, device = group_peer(k)
+                copy_small(source(q), landing.at[me], slot, device)
+
+    def send_cen(slot, peer, part=slice(None), sem=None, there=dp, sent_sem=0):
         pltpu.make_async_remote_copy(
-            src_ref=cen.at[slot, part],
+            src_ref=centres_hbm if slot is me else cen.at[slot, part],
             dst_ref=cen.at[slot, part],
-            send_sem=cen_send,
+            send_sem=cen_send.at[sent_sem],
             recv_sem=cen_recv.at[slot if sem is None else sem],
-            device_id=(dp, peer),
+            device_id=(there, peer),
             device_id_type=MESH,
         ).start()
 
@@ -149,7 +179,29 @@
     loads[1].wait()
     a_buf[me, :, 0:rows] = dir_ref[...]
     a_buf[me, :, rows : 2 * rows] = res_ref[...]
-    loads[2].wait()
+    pl.semaphore_wait(barrier, n_q + n_z + n_x - 3)
+
+    @pl.when(at_edge)
+    def _():
+        for there in served:
+            copy_small(a_buf.at[me], a_buf.at[me], 1, (there, across))
+
+    @pl.loop(1, n_q)
+    def _(k):
+        copy_small(a_buf.at[me], a_buf.at[me], 0, column_peer(k)[1])
+
+    @pl.when(at_edge)
+    def _():
+        for there in served:
+            send_cen(me, across, there=there, sent_sem=1)
+
+    send_cen(me, up)
+    send_cen(me, down)
+    send_cen(me, sibling)
+
+    @pl.loop(1, n_z)
+    def _(k):
+        pl.semaphore_signal(token, inc=1, device_id=z_peer(k), device_id_type=MESH)
 
     log2e = math.log2(math.e)
     unit = sharpness / depth * log2e
@@ -162,23 +214,7 @@
             folded = folded + square[:, other * rows : (other + 1) * rows]
         norms = jnp.sum(folded.T, axis=0, keepdims=True)
         row_term[:, part * rows : (part + 1) * rows] = (2.0 * sharpness * log2e) - unit * norms
-
-    pl.semaphore_wait(barrier, n_q + n_z + n_x - 3)
-
-    copy_small(a_buf.at[me], a_buf.at[me], 1, (dp, across))
-
-    @pl.loop(1, n_q)
-    def _(k):
-        copy_small(a_buf.at[me], a_buf.at[me], 0, column_peer(k)[1])
-
-    send_cen(me, across)
-    send_cen(me, up)
-    send_cen(me, down)
-    send_cen(me, sibling)
-
-    @pl.loop(1, n_z)
-    def _(k):
-        pl.semaphore_signal(token, inc=1, device_id=z_peer(k), device_id_type=MESH)
+    loads[2].wait()
 
     def make_tile(slot):
         tile = slot // 2
@@ -194,9 +230,15 @@
     def twin(slot):
         return slot + 1 - 2 * core
 
-    def pull(first, s):
-        low = lax.rem(first + n_ce - 4 * s, n_ce)
-        high = lax.rem(first + 4 * s, n_ce)
+    top, bottom = slice(0, rows // 2), slice(rows // 2, rows)
+    up_two = lax.rem(me + 8, n_ce)
+    down_two = lax.rem(me + n_ce - 8, n_ce)
+
+    def ends(first, s):
+        return lax.rem(first + n_ce - 4 * s, n_ce), lax.rem(first + 4 * s, n_ce)
+
+    def pull_own(s):
+        low, high = ends(me, s)
         wait_cen(low)
         if s < n_y // 2 - 1:
             send_cen(low, up)
@@ -207,19 +249,30 @@
         if s < n_y // 2 - 1:
             send_cen(high, down)
         else:
-            send_cen(high, down, bottom, n_ce + far_sem[first is across])
+            send_cen(high, down, bottom, n_ce)
         send_cen(high, sibling)
         return [low, high]
 
-    def pull_far(first):
+    def pull_across(s):
+        low, high = ends(across, s)
+        wait_cen(low)
+        if s == 2:
+            send_cen(low, up_two, top)
+            send_cen(low, up)
+        send_cen(low, sibling)
+        wait_cen(high)
+        if s == 2:
+            send_cen(high, down_two, bottom, n_ce + 1)
+            send_cen(high, down)
+        send_cen(high, sibling)
+        return [low, high]
+
+    def pull_far(first, sem):
         far = lax.rem(first + n_ce // 2, n_ce)
         wait_cen(far, top)
-        wait_cen(far, bottom, n_ce + far_sem[first is across])
+        wait_cen(far, bottom, sem)
         send_cen(far, sibling)
         return [far]
-
-    top, bottom = slice(0, rows // 2), slice(rows // 2, rows)
-    far_sem = {False: 0, True: 1}
 
     def work(slots):
         for slot in slots:
@@ -233,16 +286,16 @@
     def _(k):
         copy_small(a_buf.at[across], a_buf.at[across], 2, column_peer(k)[1])
 
-    near = pull(me, 1)
     wait_cen(across)
+    send_cen(across, up_two)
+    send_cen(across, down_two)
     send_cen(across, up)
     send_cen(across, down)
     send_cen(across, sibling)
+    near = pull_own(1)
+    work([across])
+    next_own = pull_own(2)
     work(near)
-    next_own = pull(me, 2)
-    work([across])
-    next_far = pull(across, 1)
-    work(next_own)
 
     wait_small(a_buf, n_q - 1, 0, small_recv)
     wait_small(a_buf, n_q - 1, 2, small_recv)
@@ -251,44 +304,60 @@
     for b in range(1, n_ce):
         acc = acc + fac[:, b * rows : (b + 1) * rows] * a_buf[b, :, 0:rows]
     m_buf[me] = jnp.sum(acc.T, axis=0, keepdims=True)
-
-    @pl.loop(1, n_ce)
-    def _(k):
-        copy_small(m_buf.at[me], m_buf.at[me], 3, group_peer(k)[1])
-
-    next_own = pull(me, 3)
+    push_group(3, lambda q: m_buf.at[me], m_buf)
+
+    next_far = pull_across(2)
+    work(next_own)
+    last_far = pull_across(1)
     work(next_far)
-    next_far = pull(across, 2)
-    work(next_own)
-    next_own = pull_far(me)
-    work(next_far)
-    next_far = pull(across, 3)
-    work(next_own)
-    work(next_far)
-    work(pull_far(across))
+    farther = pull_own(3)
+    work(last_far)
 
     wait_small(m_buf, n_ce - 1, 3, small_recv)
-
-    def add_weights(tile, total):
-        coeffs = jnp.concatenate([m_buf[2 * tile], m_buf[2 * tile + 1]], axis=1)
-        coeffs = jnp.broadcast_to(coeffs, (16, 2 * rows)).astype(BF16)
-        return total + jnp.dot(coeffs, tiles[tile], preferred_element_type=F32)
-
-    weights = lax.fori_loop(0, n_tiles, add_weights, jnp.zeros((16, width), F32))
+    w_acc[...] = jnp.zeros_like(w_acc)
+
+    def weigh(slots):
+        total = w_acc[...]
+        for slot in slots:
+            tile = slot // 2
+            coeffs = jnp.concatenate([m_buf[2 * tile], m_buf[2 * tile + 1]], axis=1)
+            coeffs = jnp.broadcast_to(coeffs, (16, 2 * rows)).astype(BF16)
+            total = total + jnp.dot(coeffs, tiles[tile], preferred_element_type=F32)
+        w_acc[...] = total
+
+    weigh([me, across] + near)
+    last_own = pull_across(3)
+    work(farther)
+    weigh(next_own + next_far)
+    far_across = pull_far(across, n_ce + 1)
+    work(last_own)
+    weigh(last_far + farther)
+    far_own = pull_far(me, n_ce)
+    work(far_across)
+    weigh(last_own + far_across)
+    work(far_own)
+    weigh(far_own)
+
+    weights = w_acc[...]
     upright = jnp.broadcast_to(weights[0:1], (rows, width)).T.astype(BF16)
     diagonal = lax.broadcasted_iota(jnp.int32, (rows, rows), 0) == lax.broadcasted_iota(
         jnp.int32, (rows, rows), 1
     )
 
+    across_row = weights[0:1].astype(BF16).astype(F32)
+
     @pl.loop(0, n_y)
     def _(row):
-        for side in range(2):
-            part = jnp.dot(tiles[2 * row + side], upright, preferred_element_type=F32)
-            for c in range(2):
-                picked = jnp.where(diagonal, part[c * rows : (c + 1) * rows], 0.0)
-                c_out[2 * row + c, :, side * rows : (side + 1) * rows] = jnp.sum(
-                    picked, axis=0, keepdims=True
-                )
+        part = jnp.dot(tiles[2 * row], upright, preferred_element_type=F32)
+        for c in range(2):
+            picked = jnp.where(diagonal, part[c * rows : (c + 1) * rows], 0.0)
+            c_out[2 * row + c, :, 0:rows] = jnp.sum(picked, axis=0, keepdims=True)
+            block = tiles[2 * row + 1, c * rows : (c + 1) * rows, :]
+            acc = block[:, 0:rows].astype(F32) * across_row[:, 0:rows]
+            for p in range(1, width // rows):
+                cut = slice(p * rows, (p + 1) * rows)
+                acc = acc + block[:, cut].astype(F32) * across_row[:, cut]
+            c_out[2 * row + c, :, rows : 2 * rows] = jnp.sum(acc.T, axis=0, keepdims=True)
 
     c_buf[mine] = c_out[mine]
 
@@ -315,60 +384,65 @@
     spread = jnp.broadcast_to(columns, (rows, rows)).T
     bend = m_buf[me] * columns
     for b in range(n_ce):
-        q, side = (b // 4) * 2 + b % 2, (b // 2) % 2
-        i_out[q, :, side * rows : (side + 1) * rows] = jnp.sum(
+        i_out[b // 4, :, (b % 4) * rows : (b % 4 + 1) * rows] = jnp.sum(
             fac[:, b * rows : (b + 1) * rows] * spread, axis=0, keepdims=True
         )
-        if side == 0:
-            i_out[q, :, 2 * rows : 3 * rows] = bend
-
-    @pl.loop(1, n_ce)
-    def _(k):
-        q, device = group_peer(k)
-        copy_small(i_out.at[q], i_buf.at[me], 6, device)
-
-    i_buf[me] = i_out[mine]
+    for b in range(n_y):
+        i_out[b, :, 4 * rows : 5 * rows] = bend
+
+    push_group(6, lambda q: i_out.at[q // 2], i_buf)
+
+    i_buf[me] = i_out[y]
     whole_dir = a_buf[:, :, 0:rows]
     whole_res = a_buf[:, :, rows : 2 * rows]
     dir_norm = jnp.sum(jnp.sum(whole_dir * whole_dir, axis=0), axis=1, keepdims=True)
     old_norm = jnp.sum(jnp.sum(whole_res * whole_res, axis=0), axis=1, keepdims=True)
-    pair = me - 2 * half
     wait_small(i_buf, n_ce - 1, 6, small_recv)
     summed = jnp.sum(i_buf[...], axis=0)
-    curvature = jnp.sum(summed[:, 2 * rows :], axis=1, keepdims=True) + ridge * dir_norm
+    curvature = jnp.sum(summed[:, 4 * rows :], axis=1, keepdims=True) + ridge * dir_norm
     alpha = old_norm / curvature
     squares = jnp.zeros((1, rows), F32)
-    for side in range(2):
-        own_dir = a_buf[pair + 2 * side, :, 0:rows]
-        image = summed[:, side * rows : (side + 1) * rows] + ridge * own_dir
-        left = a_buf[pair + 2 * side, :, rows : 2 * rows] - alpha * image
+    for b in range(4):
+        own_dir = a_buf[4 * y + b, :, 0:rows]
+        image = summed[:, b * rows : (b + 1) * rows] + ridge * own_dir
+        left = a_buf[4 * y + b, :, rows : 2 * rows] - alpha * image
         squares = squares + left * left
-        left_ref[side] = left
-    e_buf[mine] = squares
-
-    @pl.loop(1, n_q)
-    def _(k):
-        copy_small(e_buf.at[mine], e_buf.at[mine], 7, column_peer(k)[1])
+        left_ref[b] = left
+    e_buf[y] = squares
+
+    @pl.loop(1, n_y)
+    def _(k):
+        peer = lax.rem(me + 4 * k, n_ce)
+        copy_small(e_buf.at[y], e_buf.at[y], 7, (dp, peer))
 
     out_ref[0:1, :] = jnp.broadcast_to(alpha, (1, rows))
-    out_ref[1:2, :] = left_ref[half]
-    wait_small(e_buf, n_q - 1, 7, small_recv)
+    out_ref[1:2, :] = left_ref[me - 4 * y]
+    wait_small(e_buf, n_y - 1, 7, small_recv)
     new_norm = jnp.sum(jnp.sum(e_buf[...], axis=0), axis=1, keepdims=True)
     out_ref[2:3, :] = jnp.broadcast_to(new_norm / old_norm, (1, rows))
 
     for slot, landing, count in (
         (0, a_buf, n_q - 1),
-        (1, a_buf, 1),
         (2, a_buf, n_q - 1),
-        (3, m_buf, n_ce - 1),
+        (3, m_buf, n_q - 1 if EDGES else n_ce - 1),
         (4, c_buf, n_q - 1),
         (5, g_buf, n_p - 1),
-        (6, i_buf, n_ce - 1),
-        (7, e_buf, n_q - 1),
+        (6, i_buf, n_q - 1 if EDGES else n_ce - 1),
+        (7, e_buf, n_y - 1),
     ):
         wait_small(landing, count, slot, small_send)
-    sent = cen.at[pl.ds(0, n_ce - 1)]
-    pltpu.make_async_copy(sent, sent, cen_send).wait()
+
+    @pl.when(at_edge)
+    def _():
+        wait_small(a_buf, 2, 1, small_send)
+        if EDGES:
+            wait_small(m_buf, n_ce, 3, small_send)
+            wait_small(i_buf, n_ce, 6, small_send)
+        crossed = cen.at[pl.ds(0, 2)]
+        pltpu.make_async_copy(crossed, crossed, cen_send.at[1]).wait()
+
+    sent = cen.at[pl.ds(0, n_ce - 2)]
+    pltpu.make_async_copy(sent, sent, cen_send.at[0]).wait()
 
 
 def on_device(n_dp, n_ce, samples, centres, factor, solution, residual, direction):
@@ -398,13 +472,14 @@
             pltpu.VMEM((n_q, 1, 2 * rows), F32),
             pltpu.VMEM((2, 1, rows), F32),
             pltpu.VMEM((n_p, 1, rows), F32),
-            pltpu.VMEM((n_q, 1, 3 * rows), F32),
-            pltpu.VMEM((n_ce, 1, 3 * rows), F32),
-            pltpu.VMEM((n_q, 1, rows), F32),
-            pltpu.VMEM((2, 1, rows), F32),
+            pltpu.VMEM((n_ce // 4, 1, 5 * rows), F32),
+            pltpu.VMEM((n_ce, 1, 5 * rows), F32),
+            pltpu.VMEM((n_ce // 4, 1, rows), F32),
+            pltpu.VMEM((4, 1, rows), F32),
+            pltpu.VMEM((16, width), F32),
             pltpu.SemaphoreType.DMA((5,)),
             pltpu.SemaphoreType.DMA((n_ce + 2,)),
-            pltpu.SemaphoreType.DMA,
+            pltpu.SemaphoreType.DMA((2,)),
             pltpu.SemaphoreType.DMA((8,)),
             pltpu.SemaphoreType.DMA((8,)),
             pltpu.SemaphoreType.REGULAR,

time: 70.2 us -> 65.6 us (0.934)
  Pallas kernels: 68 us -> 63.4 us
    pallas_call x1, Pallas kernels: 68 us -> 63.4 us  [on_device(): pl.pallas_call(functools.partial(step_kernel, n_dp, n_ce, scale), out_sha...]
where the time goes in v3:
time: 65.6 us; the launch traced here: 65.4 us
  Pallas kernels  63.4 us (97%)
  other arithmetic  1.31 us (2%)
  between operations  0.67 us (1%)
    pallas_call x1, Pallas kernels, on_device(): pl.pallas_call(functools.partial(step_kernel, n_dp, n_ce, scale), out_sha...  63.4 us
    add x1, other arithmetic, on_device(): new_residual + ratio * direction  1.31 us

profile of v3, /device:TPU:1, one launch (start us, length us, event | category | flops | bytes accessed | tf_op | source)
XLA Modules:
  0.0 65.4 jit_solution(7335858597384697714)
XLA Ops:
  0.6 0.0 copy-start
  0.6 0.0 copy-start.1
  0.7 63.4 %shard_map.85 = f32[8,128]{1,0:T(8,128)} custom-call(bf16[1024,256]{1,0:T(8,128)(2,1)} %samples_hbm.1, bf16[128,256]{1,0:T(8,128)(2,1)} %centres_hbm.1, f32[128,4096]{1,0:T(8,128)} %factor_hbm.1, f32[1,128]{1,0:T(1,128)} %bitcast.14, f32[1,128]{1,0:T(1,128)} %bitcast.13), custom_call_target="tpu_custom_call" | custom-call | flops 2164260864 | bytes 2097152 | tf_op jit(solution)/shard_map/pallas_call | solution.py:456
  64.1 0.0 copy-done
  64.1 0.0 copy-done.1
  64.1 1.3 %fusion = (f32[128]{0:T(128)}, f32[128]{0:T(128)}, f32[128]{0:T(128)}) fusion(f32[128]{0:T(128)S(1)} %copy-done, f32[8,128]{1,0:T(8,128)} %shard_map.85, f32[128]{0:T(128)S(1)} %copy-done.1), kind=kLoop, calls=%fused_computation.1 | loop fusion | flops 512 | bytes 4096 | tf_op jit(solution)/shard_map/add | solution.py:497
Async XLA Ops:
  0.6 63.5 %copy-start = (f32[128]{0:T(128)S(1)}, f32[128]{0:T(128)}, u32[]{:S(2)}) copy-start(f32[128]{0:T(128)} %param.11) | copy-start | bytes 1540
  0.6 63.5 %copy-start.1 = (f32[128]{0:T(128)S(1)}, f32[128]{0:T(128)}, u32[]{:S(2)}) copy-start(f32[128]{0:T(128)} %param.9) | copy-start | bytes 1540

commit v4 on v3

--- a/solution.py
+++ b/solution.py
@@ -12,7 +12,6 @@
 ridge = 0.3
 balance = 16.0
 z_low = 4
-EDGES = True
 MESH = pl.DeviceIdType.MESH
 F32 = jnp.float32
 BF16 = jnp.bfloat16
@@ -73,6 +72,9 @@
         q = lax.rem(mine + k, n_q)
         return q, (dp, (q // 2) * 4 + half * 2 + lax.rem(q, 2))
 
+    def y_peer(k):
+        return (dp, lax.rem(me + 4 * k, n_ce))
+
     def z_peer(k):
         other = lax.rem(z + k, n_z)
         return (x * z_low + lax.rem(other, z_low), y * 4 + (other // z_low) * 2 + core)
@@ -82,10 +84,6 @@
         other = lax.rem(p, n_z)
         there = (p // n_z) * z_low + lax.rem(other, z_low)
         return other // z_low, (there, y * 4 + (other // z_low) * 2 + core)
-
-    def group_peer(k):
-        peer = lax.rem(me + k, n_ce)
-        return (peer // 4) * 2 + lax.rem(peer, 2), (dp, peer)
 
     up = lax.rem(me + 4, n_ce)
     down = lax.rem(me + n_ce - 4, n_ce)
@@ -108,10 +106,11 @@
         load.start()
 
     barrier = pltpu.get_barrier_semaphore()
-
-    @pl.loop(1, n_q)
-    def _(k):
-        pl.semaphore_signal(barrier, inc=1, device_id=column_peer(k)[1], device_id_type=MESH)
+    pl.semaphore_signal(barrier, inc=1, device_id=(dp, sibling), device_id_type=MESH)
+
+    @pl.loop(1, n_y)
+    def _(k):
+        pl.semaphore_signal(barrier, inc=1, device_id=y_peer(k), device_id_type=MESH)
 
     @pl.loop(1, n_z)
     def _(k):
@@ -137,27 +136,20 @@
         pltpu.make_async_copy(part, part, sems.at[slot]).wait()
 
     def push_group(slot, source, landing):
-        if EDGES:
-            @pl.when(at_edge)
-            def _():
-                for there in served:
-
-                    @pl.loop(0, n_q)
-                    def _(k):
-                        q = lax.rem(mine + k + n_q // 2, n_q)
-                        peer = (q // 2) * 4 + (1 - half) * 2 + lax.rem(q, 2)
-                        copy_small(source(q), landing.at[me], slot, (there, peer))
-
-            @pl.loop(1, n_q)
-            def _(k):
-                q, device = column_peer(k)
-                copy_small(source(q), landing.at[me], slot, device)
-        else:
-
-            @pl.loop(1, n_ce)
-            def _(k):
-                q, device = group_peer(k)
-                copy_small(source(q), landing.at[me], slot, device)
+        @pl.when(at_edge)
+        def _():
+            for there in served:
+
+                @pl.loop(0, n_q)
+                def _(k):
+                    q = lax.rem(mine + k + n_q // 2, n_q)
+                    peer = (q // 2) * 4 + (1 - half) * 2 + lax.rem(q, 2)
+                    copy_small(source(q), landing.at[me], slot, (there, peer))
+
+        @pl.loop(1, n_q)
+        def _(k):
+            q, device = column_peer(k)
+            copy_small(source(q), landing.at[me], slot, device)
 
     def send_cen(slot, peer, part=slice(None), sem=None, there=dp, sent_sem=0):
         pltpu.make_async_remote_copy(
@@ -179,16 +171,16 @@
     loads[1].wait()
     a_buf[me, :, 0:rows] = dir_ref[...]
     a_buf[me, :, rows : 2 * rows] = res_ref[...]
-    pl.semaphore_wait(barrier, n_q + n_z + n_x - 3)
+    pl.semaphore_wait(barrier, n_y + n_z + n_x - 2)
 
     @pl.when(at_edge)
     def _():
         for there in served:
             copy_small(a_buf.at[me], a_buf.at[me], 1, (there, across))
 
-    @pl.loop(1, n_q)
-    def _(k):
-        copy_small(a_buf.at[me], a_buf.at[me], 0, column_peer(k)[1])
+    @pl.loop(1, n_y)
+    def _(k):
+        copy_small(a_buf.at[me], a_buf.at[me], 0, y_peer(k))
 
     @pl.when(at_edge)
     def _():
@@ -282,9 +274,9 @@
     work([me])
     wait_small(a_buf, 1, 1, small_recv)
 
-    @pl.loop(1, n_q)
-    def _(k):
-        copy_small(a_buf.at[across], a_buf.at[across], 2, column_peer(k)[1])
+    @pl.loop(1, n_y)
+    def _(k):
+        copy_small(a_buf.at[across], a_buf.at[across], 2, y_peer(k))
 
     wait_cen(across)
     send_cen(across, up_two)
@@ -293,12 +285,18 @@
     send_cen(across, down)
     send_cen(across, sibling)
     near = pull_own(1)
-    work([across])
+    work([across] + near)
+    wait_small(a_buf, n_y - 1, 0, small_recv)
+    wait_small(a_buf, n_y - 1, 2, small_recv)
+
+    @pl.loop(0, n_q)
+    def _(k):
+        copy_small(a_buf.at[2 * k + core], a_buf.at[2 * k + core], 8, (dp, sibling))
+
     next_own = pull_own(2)
-    work(near)
-
-    wait_small(a_buf, n_q - 1, 0, small_recv)
-    wait_small(a_buf, n_q - 1, 2, small_recv)
+    next_far = pull_across(2)
+
+    wait_small(a_buf, n_q, 8, small_recv)
     loads[4].wait()
     acc = fac[:, 0:rows] * a_buf[0, :, 0:rows]
     for b in range(1, n_ce):
@@ -306,18 +304,19 @@
     m_buf[me] = jnp.sum(acc.T, axis=0, keepdims=True)
     push_group(3, lambda q: m_buf.at[me], m_buf)
 
-    next_far = pull_across(2)
+    last_far = pull_across(1)
     work(next_own)
-    last_far = pull_across(1)
-    work(next_far)
     farther = pull_own(3)
-    work(last_far)
+    work(next_far + last_far)
+    last_own = pull_across(3)
+    work(farther)
+    far_across = pull_far(across, n_ce + 1)
+    work(last_own)
 
     wait_small(m_buf, n_ce - 1, 3, small_recv)
-    w_acc[...] = jnp.zeros_like(w_acc)
-
-    def weigh(slots):
-        total = w_acc[...]
+
+    def weigh(slots, start=False):
+        total = jnp.zeros_like(w_acc) if start else w_acc[...]
         for slot in slots:
             tile = slot // 2
             coeffs = jnp.concatenate([m_buf[2 * tile], m_buf[2 * tile + 1]], axis=1)
@@ -325,19 +324,12 @@
             total = total + jnp.dot(coeffs, tiles[tile], preferred_element_type=F32)
         w_acc[...] = total
 
-    weigh([me, across] + near)
-    last_own = pull_across(3)
-    work(farther)
-    weigh(next_own + next_far)
-    far_across = pull_far(across, n_ce + 1)
-    work(last_own)
-    weigh(last_far + farther)
+    weigh([me, across] + near + next_own + next_far, True)
     far_own = pull_far(me, n_ce)
     work(far_across)
-    weigh(last_own + far_across)
+    weigh(last_far + farther + last_own)
     work(far_own)
-    weigh(far_own)
-
+    weigh(far_across + far_own)
     weights = w_acc[...]
     upright = jnp.broadcast_to(weights[0:1], (rows, width)).T.astype(BF16)
     diagonal = lax.broadcasted_iota(jnp.int32, (rows, rows), 0) == lax.broadcasted_iota(
@@ -346,8 +338,12 @@
 
     across_row = weights[0:1].astype(BF16).astype(F32)
 
+    def far_first(k):
+        return lax.rem(y + n_y // 2 + (k + 1) // 2 * (1 - 2 * lax.rem(k, 2)), n_y)
+
     @pl.loop(0, n_y)
-    def _(row):
+    def _(k):
+        row = far_first(k)
         part = jnp.dot(tiles[2 * row], upright, preferred_element_type=F32)
         for c in range(2):
             picked = jnp.where(diagonal, part[c * rows : (c + 1) * rows], 0.0)
@@ -358,14 +354,14 @@
                 cut = slice(p * rows, (p + 1) * rows)
                 acc = acc + block[:, cut].astype(F32) * across_row[:, cut]
             c_out[2 * row + c, :, rows : 2 * rows] = jnp.sum(acc.T, axis=0, keepdims=True)
+        there = row * 4 + half * 2
+        copy_small(c_out.at[2 * row + 1 - core], c_buf.at[mine], 4, (dp, there + 1 - core))
+
+        @pl.when(row != y)
+        def _():
+            copy_small(c_out.at[2 * row + core], c_buf.at[mine], 4, (dp, there + core))
 
     c_buf[mine] = c_out[mine]
-
-    @pl.loop(1, n_q)
-    def _(k):
-        q, device = column_peer(k)
-        copy_small(c_out.at[q], c_buf.at[mine], 4, device)
-
     wait_small(c_buf, n_q - 1, 4, small_recv)
     both = jnp.sum(c_buf[...], axis=0)
     g_out[0] = both[:, 0:rows]
@@ -383,14 +379,29 @@
 
     spread = jnp.broadcast_to(columns, (rows, rows)).T
     bend = m_buf[me] * columns
-    for b in range(n_ce):
-        i_out[b // 4, :, (b % 4) * rows : (b % 4 + 1) * rows] = jnp.sum(
-            fac[:, b * rows : (b + 1) * rows] * spread, axis=0, keepdims=True
-        )
-    for b in range(n_y):
-        i_out[b, :, 4 * rows : 5 * rows] = bend
-
-    push_group(6, lambda q: i_out.at[q // 2], i_buf)
+    @pl.loop(0, n_y)
+    def _(k):
+        row = far_first(k)
+        for b in range(4):
+            start = pl.multiple_of((4 * row + b) * rows, rows)
+            i_out[row, :, b * rows : (b + 1) * rows] = jnp.sum(
+                fac[:, pl.ds(start, rows)] * spread, axis=0, keepdims=True
+            )
+        i_out[row, :, 4 * rows : 5 * rows] = bend
+
+        @pl.when(at_edge)
+        def _():
+            for there in served:
+                for c in range(2):
+                    peer = row * 4 + (1 - half) * 2 + c
+                    copy_small(i_out.at[row], i_buf.at[me], 6, (there, peer))
+
+        near_by = row * 4 + half * 2
+        copy_small(i_out.at[row], i_buf.at[me], 6, (dp, near_by + 1 - core))
+
+        @pl.when(row != y)
+        def _():
+            copy_small(i_out.at[row], i_buf.at[me], 6, (dp, near_by + core))
 
     i_buf[me] = i_out[y]
     whole_dir = a_buf[:, :, 0:rows]
@@ -422,12 +433,13 @@
     out_ref[2:3, :] = jnp.broadcast_to(new_norm / old_norm, (1, rows))
 
     for slot, landing, count in (
-        (0, a_buf, n_q - 1),
-        (2, a_buf, n_q - 1),
-        (3, m_buf, n_q - 1 if EDGES else n_ce - 1),
+        (0, a_buf, n_y - 1),
+        (2, a_buf, n_y - 1),
+        (8, a_buf, n_q),
+        (3, m_buf, n_q - 1),
         (4, c_buf, n_q - 1),
         (5, g_buf, n_p - 1),
-        (6, i_buf, n_q - 1 if EDGES else n_ce - 1),
+        (6, i_buf, n_q - 1),
         (7, e_buf, n_y - 1),
     ):
         wait_small(landing, count, slot, small_send)
@@ -435,9 +447,8 @@
     @pl.when(at_edge)
     def _():
         wait_small(a_buf, 2, 1, small_send)
-        if EDGES:
-            wait_small(m_buf, n_ce, 3, small_send)
-            wait_small(i_buf, n_ce, 6, small_send)
+        wait_small(m_buf, n_ce, 3, small_send)
+        wait_small(i_buf, n_ce, 6, small_send)
         crossed = cen.at[pl.ds(0, 2)]
         pltpu.make_async_copy(crossed, crossed, cen_send.at[1]).wait()
 
@@ -480,8 +491,8 @@
             pltpu.SemaphoreType.DMA((5,)),
             pltpu.SemaphoreType.DMA((n_ce + 2,)),
             pltpu.SemaphoreType.DMA((2,)),
-            pltpu.SemaphoreType.DMA((8,)),
-            pltpu.SemaphoreType.DMA((8,)),
+            pltpu.SemaphoreType.DMA((9,)),
+            pltpu.SemaphoreType.DMA((9,)),
             pltpu.SemaphoreType.REGULAR,
         ],
         compiler_params=pltpu.CompilerParams(

time: 65.6 us -> 62.9 us (0.959)
  Pallas kernels: 63.4 us -> 60.7 us
    pallas_call x1, Pallas kernels: 63.4 us -> 60.7 us  [on_device(): pl.pallas_call(functools.partial(step_kernel, n_dp, n_ce, scale), out_sha...]
where the time goes in v4:
time: 62.9 us; the launch traced here: 62.7 us
  Pallas kernels  60.7 us (97%)
  other arithmetic  1.31 us (2%)
  between operations  0.67 us (1%)
    pallas_call x1, Pallas kernels, on_device(): pl.pallas_call(functools.partial(step_kernel, n_dp, n_ce, scale), out_sha...  60.7 us
    add x1, other arithmetic, on_device(): new_residual + ratio * direction  1.31 us

profile of v4, /device:TPU:1, one launch (start us, length us, event | category | flops | bytes accessed | tf_op | source)
XLA Modules:
  0.0 62.7 jit_solution(6141779700809980092)
XLA Ops:
  0.6 0.0 copy-start
  0.6 0.0 copy-start.1
  0.7 60.7 %shard_map.85 = f32[8,128]{1,0:T(8,128)} custom-call(bf16[1024,256]{1,0:T(8,128)(2,1)} %samples_hbm.1, bf16[128,256]{1,0:T(8,128)(2,1)} %centres_hbm.1, f32[128,4096]{1,0:T(8,128)} %factor_hbm.1, f32[1,128]{1,0:T(1,128)} %bitcast.14, f32[1,128]{1,0:T(1,128)} %bitcast.13), custom_call_target="tpu_custom_call" | custom-call | flops 2164260864 | bytes 2097152 | tf_op jit(solution)/shard_map/pallas_call | solution.py:467
  61.4 0.0 copy-done
  61.4 0.0 copy-done.1
  61.4 1.3 %fusion = (f32[128]{0:T(128)}, f32[128]{0:T(128)}, f32[128]{0:T(128)}) fusion(f32[128]{0:T(128)S(1)} %copy-done, f32[8,128]{1,0:T(8,128)} %shard_map.85, f32[128]{0:T(128)S(1)} %copy-done.1), kind=kLoop, calls=%fused_computation.1 | loop fusion | flops 512 | bytes 4096 | tf_op jit(solution)/shard_map/add | solution.py:508
Async XLA Ops:
  0.6 60.7 %copy-start = (f32[128]{0:T(128)S(1)}, f32[128]{0:T(128)}, u32[]{:S(2)}) copy-start(f32[128]{0:T(128)} %param.11) | copy-start | bytes 1540
  0.6 60.7 %copy-start.1 = (f32[128]{0:T(128)S(1)}, f32[128]{0:T(128)}, u32[]{:S(2)}) copy-start(f32[128]{0:T(128)} %param.9) | copy-start | bytes 1540

commit v5 on v4

--- a/solution.py
+++ b/solution.py
@@ -80,9 +80,11 @@
         return (x * z_low + lax.rem(other, z_low), y * 4 + (other // z_low) * 2 + core)
 
     def plane_peer(k):
-        p = lax.rem(place + k, n_p)
-        other = lax.rem(p, n_z)
-        there = (p // n_z) * z_low + lax.rem(other, z_low)
+        step = k // n_x
+        move = n_z // 2 + (step + 1) // 2 * (1 - 2 * lax.rem(step, 2))
+        other = lax.rem(z + move, n_z)
+        other_x = lax.rem(x + lax.rem(k, n_x) + 1, n_x)
+        there = other_x * z_low + lax.rem(other, z_low)
         return other // z_low, (there, y * 4 + (other // z_low) * 2 + core)
 
     up = lax.rem(me + 4, n_ce)
@@ -148,7 +150,8 @@
 
         @pl.loop(1, n_q)
         def _(k):
-            q, device = column_peer(k)
+            move = n_q // 2 + (k // 2) * (1 - 2 * lax.rem(k, 2))
+            q, device = column_peer(lax.rem(move, n_q))
             copy_small(source(q), landing.at[me], slot, device)
 
     def send_cen(slot, peer, part=slice(None), sem=None, there=dp, sent_sem=0):
@@ -311,7 +314,8 @@
     last_own = pull_across(3)
     work(farther)
     far_across = pull_far(across, n_ce + 1)
-    work(last_own)
+    far_own = pull_far(me, n_ce)
+    work(last_own + far_across)
 
     wait_small(m_buf, n_ce - 1, 3, small_recv)
 
@@ -325,8 +329,6 @@
         w_acc[...] = total
 
     weigh([me, across] + near + next_own + next_far, True)
-    far_own = pull_far(me, n_ce)
-    work(far_across)
     weigh(last_far + farther + last_own)
     work(far_own)
     weigh(far_across + far_own)
@@ -368,7 +370,7 @@
     g_out[1] = both[:, rows : 2 * rows]
     pl.semaphore_wait(token, n_z - 1)
 
-    @pl.loop(1, n_p)
+    @pl.loop(0, n_p - 1)
     def _(k):
         side, device = plane_peer(k)
         copy_small(g_out.at[side], g_buf.at[place], 5, device)

time: 62.9 us -> 62.2 us (0.989)
    pallas_call x1, Pallas kernels: 60.7 us -> 60.1 us  [on_device(): pl.pallas_call(functools.partial(step_kernel, n_dp, n_ce, scale), out_sha...]
where the time goes in v5:
time: 62.2 us; the launch traced here: 62.1 us
  Pallas kernels  60.1 us (97%)
  other arithmetic  1.31 us (2%)
  between operations  0.67 us (1%)
    pallas_call x1, Pallas kernels, on_device(): pl.pallas_call(functools.partial(step_kernel, n_dp, n_ce, scale), out_sha...  60.1 us
    add x1, other arithmetic, on_device(): new_residual + ratio * direction  1.31 us

profile of v5, /device:TPU:1, one launch (start us, length us, event | category | flops | bytes accessed | tf_op | source)
XLA Modules:
  0.0 62.1 jit_solution(1805280365549833537)
XLA Ops:
  0.6 0.0 copy-start
  0.6 0.0 copy-start.1
  0.7 60.1 %shard_map.85 = f32[8,128]{1,0:T(8,128)} custom-call(bf16[1024,256]{1,0:T(8,128)(2,1)} %samples_hbm.1, bf16[128,256]{1,0:T(8,128)(2,1)} %centres_hbm.1, f32[128,4096]{1,0:T(8,128)} %factor_hbm.1, f32[1,128]{1,0:T(1,128)} %bitcast.14, f32[1,128]{1,0:T(1,128)} %bitcast.13), custom_call_target="tpu_custom_call" | custom-call | flops 2164260864 | bytes 2097152 | tf_op jit(solution)/shard_map/pallas_call | solution.py:469
  60.7 0.0 copy-done
  60.7 0.0 copy-done.1
  60.7 1.3 %fusion = (f32[128]{0:T(128)}, f32[128]{0:T(128)}, f32[128]{0:T(128)}) fusion(f32[128]{0:T(128)S(1)} %copy-done, f32[8,128]{1,0:T(8,128)} %shard_map.85, f32[128]{0:T(128)S(1)} %copy-done.1), kind=kLoop, calls=%fused_computation.1 | loop fusion | flops 512 | bytes 4096 | tf_op jit(solution)/shard_map/add | solution.py:510
Async XLA Ops:
  0.6 60.1 %copy-start = (f32[128]{0:T(128)S(1)}, f32[128]{0:T(128)}, u32[]{:S(2)}) copy-start(f32[128]{0:T(128)} %param.11) | copy-start | bytes 1540
  0.6 60.1 %copy-start.1 = (f32[128]{0:T(128)S(1)}, f32[128]{0:T(128)}, u32[]{:S(2)}) copy-start(f32[128]{0:T(128)} %param.9) | copy-start | bytes 1540
